TPU v7x, 256 devices: a whole 4x4x8 slice. The times are simulated.
256 devices in a mesh: az: 32 (over y, z), rg: 8 (over x, core).
Axes of the slice: x: 4, y: 4, z: 8, core: 2. Of those that a mesh axis runs over, the one named last changes fastest.
Arguments:
- echo_field: float32 [2, 2048, 8192], P(None, 'az', 'rg'), may hold values from -6 to 6
- range_chirp: bfloat16 [2, 2048], replicated, may hold values from -0.25 to 0.25
- azimuth_filter: float32 [2, 2048, 8192], P(None, 'az', 'rg'), may hold values from -5 to 5
- shifts: int32 [2048], P('az'), may hold values from 0 to 2040, as said below
- tap_index: int32 [2048], P('az'), may hold values from 0 to 15
- taps_table: float32 [16, 8], replicated, may hold values from -2 to 2
Outputs:
- focused_image: float32 [2, 2048, 8192], P(None, 'az', 'rg')
Inputs may be any that keep to these rules, and one draw needn't show every extreme that they name: Within each aligned block of 64 rows at most 32 shifts are 1024 or more, and some block has exactly 32; a shift below 1024 is at most 1016, any other at most 2040.
All inputs are finite; a program needn't handle non-finite values.
Results may differ from a plain program's by a relative error of at most 0.0029.
Values may be sent and summed in bfloat16 or wider, within the bound.
A program may use at most 128 MiB of HBM per device.

v0:
```python
import functools
import math

import jax
import jax.numpy as jnp
import numpy as np
from jax import lax
from jax.experimental import pallas as pl
from jax.experimental.pallas import tpu as pltpu
from jax.sharding import PartitionSpec as P

MESH = pl.DeviceIdType.MESH
F32 = jnp.float32
BF16 = jnp.bfloat16
LANE = 128
SUB = 16
HALF = 8
PARTS = 4
JOBS = 2
PASSED = 3
UNROLL = 4


def encode(x):
    return (x * jnp.abs(x)).astype(BF16)


def decode(code):
    c = code.astype(F32)
    return c * lax.rsqrt(jnp.maximum(jnp.abs(c), 1e-37))


def bit_reverse(value, bits):
    result = 0
    for position in range(bits):
        result += ((value >> position) & 1) << (bits - 1 - position)
    return result


def turn(pair, k, n, sign):
    re, im = pair
    if k == 0:
        return re, im
    if 4 * k == n:
        return (-im, re) if sign > 0 else (im, -re)
    c = math.cos(2 * math.pi * k / n)
    s = sign * math.sin(2 * math.pi * k / n)
    if 8 * k == n:
        return ((re - im) * c, (re + im) * c) if sign > 0 else ((re + im) * c, (im - re) * c)
    if 8 * k == 3 * n:
        h = -c
        return (-(re + im) * h, (re - im) * h) if sign > 0 else ((im - re) * h, -(re + im) * h)
    return re * c - im * s, re * s + im * c


def fft_forward(xs):
    n = len(xs)
    if n == 1:
        return xs
    half = n // 2
    low, high = [], []
    for k in range(half):
        (ar, ai), (br, bi) = xs[k], xs[k + half]
        low.append((ar + br, ai + bi))
        high.append(turn((ar - br, ai - bi), k, n, -1))
    return fft_forward(low) + fft_forward(high)


def fft_inverse(xs):
    n = len(xs)
    if n == 1:
        return xs
    half = n // 2
    low = fft_inverse(xs[:half])
    high = fft_inverse(xs[half:])
    first, second = [], []
    for k in range(half):
        ar, ai = low[k]
        br, bi = turn(high[k], k, n, 1)
        first.append((ar + br, ai + bi))
        second.append((ar - br, ai - bi))
    return first + second


def packed(rows):
    group, part, inner = np.meshgrid(
        np.arange(rows // HALF), np.arange(2), np.arange(HALF), indexing="ij"
    )
    return (part * rows + group * HALF + inner).reshape(-1)


def trig_tables(n_az, rows):
    total = n_az * rows
    bits = n_az.bit_length() - 1
    order = packed(rows)
    tables = np.zeros((n_az, 4, 2 * rows, 2 * rows), np.float32)
    s = np.arange(rows)[None, :]
    j = np.arange(rows)[:, None]
    for p in range(n_az):
        b = bit_reverse(p, bits)
        angle = 2 * np.pi * ((s * (b + n_az * j)) % total) / total
        c, d = np.cos(angle) / math.sqrt(rows), np.sin(angle) / math.sqrt(rows)
        m = np.block([[c, d], [-d, c]])[np.ix_(order, order)]
        for at, mat in ((0, m), (2, m.T)):
            high = mat.astype(np.float32).astype(jnp.bfloat16)
            tables[p, at] = high.astype(np.float32)
            tables[p, at + 1] = mat - high.astype(np.float64)
    return tables.astype(jnp.bfloat16)


def kernel(
    n,
    ng,
    slots,
    echo_hbm,
    chirp_hbm,
    filt_hbm,
    shifts_hbm,
    tap_index_hbm,
    table_hbm,
    trig_hbm,
    out,
    echo,
    chirp,
    filt,
    shifts,
    tap_index,
    table,
    trig,
    band,
    weights,
    wide,
    shift_wide,
    coef_wide,
    spread,
    gathering,
    send_1,
    recv_1,
    send_2,
    recv_2,
    spec,
    spec_code,
    far_code,
    halo_1,
    halo_2,
    high,
    low,
    send_3,
    recv_3,
    send_4,
    recv_4,
    local_sem,
    halo_send,
    halo_recv,
    pass_send,
    part_send,
    part_recv,
    job_send,
    job_recv,
):
    rows, cells = echo.shape[1], echo.shape[2]
    chirp_len = chirp.shape[1]
    part = cells // PARTS
    lanes = part // LANE
    groups = rows // HALF
    block = 256
    nz = 8
    me = lax.axis_index("az")
    g = lax.axis_index("rg")

    def fetch(src, dst, at):
        copy = pltpu.make_async_copy(src, dst, local_sem.at[at])
        copy.start()
        return copy

    echo_copy = fetch(echo_hbm, echo, 0)
    chirp_copy = fetch(chirp_hbm, chirp, 1)
    shifts_copy = fetch(shifts_hbm, shifts, 2)
    index_copy = fetch(tap_index_hbm, tap_index, 3)
    table_copy = fetch(table_hbm, table, 4)
    trig_copy = fetch(trig_hbm.at[me], trig, 5)
    filt_copy = fetch(filt_hbm, filt, 6)

    barrier = pltpu.get_barrier_semaphore()

    def greet(k, carry):
        pl.semaphore_signal(
            barrier, inc=1, device_id=(lax.rem(me + k, n), g), device_id_type=MESH
        )
        return carry

    lax.fori_loop(1, n, greet, 0)
    for d in (1, 2, ng - 2, ng - 1):
        pl.semaphore_signal(barrier, inc=1, device_id=(me, lax.rem(g + d, ng)), device_id_type=MESH)

    echo_copy.wait()
    for s in range(groups):
        at = slice(HALF * s, HALF * (s + 1))
        wide[SUB * s : SUB * (s + 1), 0:cells] = jnp.concatenate(
            [echo[0, at, :], echo[1, at, :]], axis=0
        ).astype(BF16)

    pl.semaphore_wait(barrier, n - 1 + 4)

    def halo_copy(src, dst, slot, d):
        return pltpu.make_async_remote_copy(
            src_ref=src,
            dst_ref=dst,
            send_sem=halo_send.at[slot],
            recv_sem=halo_recv.at[slot],
            device_id=(me, lax.rem(g - d + ng, ng)),
            device_id_type=MESH,
        )

    odd = lax.rem(g, 2) == 1

    def sends_echo(d, h):
        far_enough = g >= d
        return far_enough & odd if d == 2 and h < PASSED else far_enough

    def pass_on(h):
        return pltpu.make_async_remote_copy(
            src_ref=wide.at[:, pl.ds(cells + part * h, part)],
            dst_ref=wide.at[:, pl.ds(2 * cells + part * h, part)],
            send_sem=pass_send.at[h],
            recv_sem=halo_recv.at[PARTS + h],
            device_id=(me, lax.rem(g - 1 + ng, ng)),
            device_id_type=MESH,
        )

    passes_on = odd & (g + 1 < ng)

    def echo_copy_of(d, h):
        return halo_copy(
            wide.at[:, pl.ds(part * h, part)],
            wide.at[:, pl.ds(d * cells + part * h, part)],
            PARTS * (d - 1) + h,
            d,
        )

    for d in (1, 2):
        for h in range(PARTS):
            pl.when(sends_echo(d, h))(echo_copy_of(d, h).start)

    chirp_copy.wait()
    span = chirp_len + 2 * block
    row_id = lax.broadcasted_iota(jnp.int32, (LANE, LANE), 0)
    col_id = lax.broadcasted_iota(jnp.int32, (LANE, LANE), 1)
    mirror = (row_id + col_id == LANE - 1).astype(BF16)
    pieces = [
        jnp.dot(chirp[:, LANE * i : LANE * (i + 1)], mirror, preferred_element_type=F32)
        for i in reversed(range(chirp_len // LANE))
    ]
    edge = jnp.zeros((2, block), F32)
    base = jnp.concatenate([edge] + pieces + [edge], axis=1)
    for c in range(2):
        copies = jnp.broadcast_to(base[c : c + 1], (LANE, span))
        band[c] = pltpu.roll(copies, 1, 1, stride=1, stride_axis=0).astype(BF16)
    for a in range((chirp_len + block) // LANE):
        start = chirp_len + block - LANE * a
        for c in range(2):
            weights[LANE * a : LANE * (a + 1), block * c : block * (c + 1)] = band[
                c, :, start : start + block
            ]

    shifts_copy.wait()
    index_copy.wait()
    table_copy.wait()
    phases = table.shape[1]
    on_row = lax.broadcasted_iota(jnp.int32, (2 * rows, rows), 0)
    on_col = lax.broadcasted_iota(jnp.int32, (2 * rows, rows), 1)
    row_of = lax.div(on_row, SUB) * HALF + lax.rem(on_row, HALF)

    def across(values):
        return jnp.broadcast_to(values.astype(F32).reshape(1, rows), (2 * rows, rows))

    def pick(mask, values):
        return jnp.sum(jnp.where(mask, values, 0.0), axis=1, keepdims=True)

    shift_row = across(shifts[...])
    shift = pick(row_of == on_col, shift_row)
    distant = shift >= float(cells)
    rank = pick(on_col < row_of, jnp.where(shift_row >= float(cells), 1.0, 0.0))
    plain_row = lax.broadcasted_iota(jnp.int32, (rows, rows), 0)
    plain_col = lax.broadcasted_iota(jnp.int32, (rows, rows), 1)

    def upright(values):
        spread_out = jnp.broadcast_to(values.astype(F32).reshape(1, rows), (rows, rows))
        return pick(plain_row == plain_col, spread_out)

    shift_wide[...] = jnp.broadcast_to(upright(shifts[...]).astype(jnp.int32), (rows, LANE))
    phase_id = lax.broadcasted_iota(jnp.int32, (rows, phases), 1).astype(F32)
    coefs = lax.dot_general(
        jnp.where(upright(tap_index[...]) == phase_id, 1.0, 0.0),
        table[...],
        (((1,), (1,)), ((), ())),
        precision=lax.Precision.HIGHEST,
        preferred_element_type=F32,
    )
    for q in range(coef_wide.shape[0]):
        coef_wide[q] = jnp.broadcast_to(coefs[:, q : q + 1], (rows, LANE))
    from_row = lax.broadcasted_iota(jnp.int32, (2 * rows, 2 * slots), 0)
    to_slot = lax.broadcasted_iota(jnp.int32, (2 * rows, 2 * slots), 1)
    same_part = lax.rem(lax.div(from_row, HALF), 2) == lax.rem(lax.div(to_slot, HALF), 2)
    slot_of = (lax.div(to_slot, SUB) * HALF + lax.rem(to_slot, HALF)).astype(F32)
    matches = jnp.where(rank == slot_of, 1.0, 0.0) * jnp.where(same_part, 1.0, 0.0)
    matches = matches * jnp.where(distant, 1.0, 0.0)
    spread[...] = matches.astype(BF16)
    gathering[...] = matches.T.astype(BF16)

    ny = n // nz
    my_y, my_z = lax.div(me, nz), lax.rem(me, nz)
    parity = lax.rem(me, 2)
    spot = my_y * (nz // 2) + lax.div(my_z, 2)

    def away(i, count):
        return count // 2 + (1 - 2 * lax.rem(i, 2)) * lax.div(i + 1, 2)

    def tile(ref, p, at):
        row = pl.multiple_of(SUB * lax.div(at, lanes), SUB)
        col = pl.multiple_of(LANE * lax.rem(at, lanes), LANE)
        return ref.at[p, pl.ds(row, SUB), pl.ds(col, LANE)]

    def other(p):
        return lax.rem(parity + p, 2)

    def scatter(src, dst, phase, p):
        job = p // JOBS

        def start(k, carry):
            y = lax.rem(my_y + away(lax.rem(k, ny), ny), ny)
            z = lax.rem(my_z + 2 * away(lax.div(k, ny), nz // 2) + other(p), nz)
            pltpu.make_async_remote_copy(
                src_ref=tile(src, p, y * (nz // 2) + lax.div(z, 2)),
                dst_ref=dst.at[job, me],
                send_sem=part_send.at[phase, p],
                recv_sem=job_recv.at[phase, job],
                device_id=(y * nz + z, g),
                device_id_type=MESH,
            ).start()
            return carry

        lax.fori_loop(0, n // 2 - 1 + other(p), start, 0)

        @pl.when(other(p) == 0)
        def _():
            pltpu.make_async_copy(
                tile(src, p, spot), dst.at[job, me], job_recv.at[phase, job]
            ).start()

    def gather(src, dst, phase, job):
        p = 2 * job + parity

        def start(k, carry):
            y = lax.rem(my_y + away(lax.rem(k, ny), ny), ny)
            z = lax.rem(my_z + away(lax.div(k, ny), nz), nz)
            q = y * nz + z
            pltpu.make_async_remote_copy(
                src_ref=src.at[job, q],
                dst_ref=tile(dst, p, spot),
                send_sem=job_send.at[phase, job],
                recv_sem=part_recv.at[phase, p],
                device_id=(q, g),
                device_id_type=MESH,
            ).start()
            return carry

        lax.fori_loop(0, n - 1, start, 0)
        pltpu.make_async_copy(src.at[job, me], tile(dst, p, spot), part_recv.at[phase, p]).start()

    def scattered(dst, phase, job):
        pltpu.make_async_copy(dst.at[job], dst.at[job], job_recv.at[phase, job]).wait()

    def gathered(dst, phase, p):
        pltpu.make_async_copy(dst.at[p], dst.at[p], part_recv.at[phase, p]).wait()

    def transform(fft, src, dst, h):
        xs = []
        for p in range(n):
            value = decode(src[h, p])
            xs.append((value[:HALF], value[HALF:]))
        for p, (re, im) in enumerate(fft(xs)):
            dst[h, p] = encode(jnp.concatenate([re, im], axis=0) * (1.0 / math.sqrt(n)))

    def compress(h):
        left = wide[:, part * h : part * h + chirp_len + block]
        product = jnp.dot(left, weights[...], preferred_element_type=F32)
        piece = product.reshape(groups, 2, HALF, 2 * block)
        real = piece[:, 0, :, :block] - piece[:, 1, :, block:]
        imag = piece[:, 0, :, block:] + piece[:, 1, :, :block]
        send_1[h] = encode(jnp.concatenate([real, imag], axis=1).reshape(2 * rows, block))

    def echo_arrived(d, h):
        pl.when(g + d < ng)(echo_copy_of(d, h).wait_recv)

        @pl.when(g + d >= ng)
        def _():
            start = d * cells + part * h
            wide[:, start : start + part] = jnp.zeros((2 * rows, part), BF16)

    for h in range(PARTS):
        echo_arrived(1, h)
        if h < PASSED:
            pl.when(passes_on)(pass_on(h).start)
    for h in range(PARTS):
        echo_arrived(2, h)
        compress(h)
        scatter(send_1, recv_1, 0, h)

    for job in range(JOBS):
        scattered(recv_1, 0, job)
        transform(fft_forward, recv_1, send_2, job)
        gather(send_2, recv_2, 0, job)

    def times(at, upper, lower):
        return jnp.dot(
            jnp.concatenate([trig[at], trig[at + 1], trig[at]], axis=1),
            jnp.concatenate([upper, upper, lower], axis=0),
            preferred_element_type=F32,
        )

    def split(value):
        upper = value.astype(BF16)
        return upper, (value - upper.astype(F32)).astype(BF16)

    def spec_copy_of(d, h):
        src, dst = ((spec_code, halo_1), (far_code, halo_2))[d - 1]
        return halo_copy(src.at[h], dst.at[h], 2 * PARTS + PARTS * (d - 1) + h, d)

    trig_copy.wait()
    for h in range(PARTS):
        gathered(recv_2, 0, h)
        spectrum = times(0, *split(decode(recv_2[h])))
        code = encode(spectrum)
        spec_code[h] = code
        pl.when(g >= 1)(spec_copy_of(1, h).start)
        far_code[h] = jnp.dot(gathering[...], code, preferred_element_type=F32).astype(BF16)
        pl.when(g >= 2)(spec_copy_of(2, h).start)
        spec[:, part * h : part * (h + 1)] = spectrum

    def spec_arrived(d, h):
        dst = (halo_1, halo_2)[d - 1]
        pl.when(g + d < ng)(spec_copy_of(d, h).wait_recv)

        @pl.when(g + d >= ng)
        def _():
            dst[h] = jnp.zeros(dst.shape[1:], BF16)

        start = d * cells + part * h
        if d == 1:
            value = halo_1[h]
        else:
            value = jnp.dot(spread[...], halo_2[h], preferred_element_type=F32)
        spec[:, start : start + part] = decode(value)


    lane = lax.broadcasted_iota(jnp.int32, (HALF, LANE), 1)
    block_tiles = cells // LANE
    reach = cells // 2
    lanes_out = reach // LANE

    def ahead(xs, by):
        moved = [pltpu.roll(x, LANE - by, 1) for x in xs]
        kept = lane < LANE - by
        return [jnp.where(kept, a, b) for a, b in zip(moved, moved[1:])] + [moved[-1]]

    def migrate(h):
        start = reach * h

        def row_group(j):
            at = pl.multiple_of(SUB * j, SUB)
            own = pl.multiple_of(HALF * j, HALF)
            shift = shift_wide[pl.ds(own, HALF), :]
            distant = shift >= cells
            rest = jnp.where(distant, shift - cells, shift)
            fine = rest & (LANE - 1)
            turned = lane + fine
            inside = turned < LANE
            turned = jnp.where(inside, turned, turned - LANE)
            totals = []
            for c in range(2):
                row = pl.ds(pl.multiple_of(at + HALF * c, HALF), HALF)

                def load(t):
                    return spec[row, start + LANE * t : start + LANE * (t + 1)]

                count = lanes_out + block_tiles
                cur = [
                    jnp.where(distant, load(t + block_tiles), load(t)) for t in range(count)
                ]
                step = block_tiles // 2
                while step >= 1:
                    bit = (rest & (step * LANE)) != 0
                    width = lanes_out + step + 1
                    cur = [
                        jnp.where(bit, cur[min(t + step, count - 1)], cur[t]) for t in range(width)
                    ]
                    count = width
                    step //= 2
                cur = [jnp.take_along_axis(x, turned, axis=1) for x in cur]
                cur = [jnp.where(inside, cur[t], cur[t + 1]) for t in range(lanes_out + 1)]
                weight = [coef_wide[q, pl.ds(own, HALF), :] for q in range(8)]
                four = ahead(cur, 4)
                pair = [
                    [weight[q] * x + weight[q + 4] * y for x, y in zip(cur, four)]
                    for q in range(4)
                ]
                even = [x + y for x, y in zip(pair[0], ahead(pair[2], 2))]
                odd = [x + y for x, y in zip(pair[1], ahead(pair[3], 2))]
                total = [x + y for x, y in zip(even, ahead(odd, 1))]
                totals.append(total)
            for t in range(lanes_out):
                col = slice(start + LANE * t, start + LANE * (t + 1))
                fr = filt[0, pl.ds(own, HALF), col]
                fi = filt[1, pl.ds(own, HALF), col]
                x, y = totals[0][t], totals[1][t]
                both = jnp.concatenate([x * fr - y * fi, x * fi + y * fr], axis=0)
                upper, lower = split(both)
                high[pl.ds(at, SUB), col] = upper
                low[pl.ds(at, SUB), col] = lower

        def some(j, carry):
            for u in range(UNROLL):
                row_group(UNROLL * j + u)
            return carry

        lax.fori_loop(0, groups // UNROLL, some, 0)

    for h in range(PARTS):
        spec_arrived(1, h)
    filt_copy.wait()
    for half in range(2):
        for h in range(PARTS // 2 * half, PARTS // 2 * (half + 1)):
            spec_arrived(2, h)
        migrate(half)
        for h in range(PARTS // 2 * half, PARTS // 2 * (half + 1)):
            col = slice(part * h, part * (h + 1))
            send_3[h] = encode(times(2, high[:, col], low[:, col]))
            scatter(send_3, recv_3, 1, h)

    for job in range(JOBS):
        scattered(recv_3, 1, job)
        transform(fft_inverse, recv_3, send_4, job)
        gather(send_4, recv_4, 1, job)
    for h in range(PARTS):
        gathered(recv_4, 1, h)
        for s in range(groups):
            value = decode(recv_4[h, SUB * s : SUB * (s + 1), :])
            for c in range(2):
                out[c, HALF * s : HALF * (s + 1), part * h : part * (h + 1)] = value[
                    HALF * c : HALF * (c + 1)
                ]

    for h in range(PASSED):
        pl.when(passes_on)(pass_on(h).wait_send)
    for d in (1, 2):
        for h in range(PARTS):
            pl.when(sends_echo(d, h))(echo_copy_of(d, h).wait_send)
            pl.when(g >= d)(spec_copy_of(d, h).wait_send)
    for phase in range(2):
        for job in range(JOBS):
            sent = send_2.at[0, pl.ds(0, n - 1)]
            pltpu.make_async_copy(sent, sent, job_send.at[phase, job]).wait()
        for p in range(PARTS):
            for same in (0, 1):
                sent = send_2.at[0, pl.ds(0, n // 2 - 1 + same)]
                pl.when(other(p) == same)(
                    pltpu.make_async_copy(sent, sent, part_send.at[phase, p]).wait
                )


def solution(mesh):
    n, ng = mesh.shape["az"], mesh.shape["rg"]

    def local(echo_field, range_chirp, azimuth_filter, shifts, tap_index, taps_table):
        rows, cells = echo_field.shape[1], echo_field.shape[2]
        chirp_len = range_chirp.shape[1]
        phases, taps = taps_table.shape
        block = 256
        slots = rows // 2
        part = cells // PARTS
        trig = jnp.asarray(trig_tables(n, rows))
        stack = (2, rows, cells)
        flat = (PARTS, 2 * rows, part)
        tiles = (JOBS, n, SUB, LANE)
        hbm = pl.BlockSpec(memory_space=pltpu.HBM)
        return pl.pallas_call(
            functools.partial(kernel, n, ng, slots),
            out_shape=pltpu.VMEM(stack, F32),
            in_specs=[hbm] * 7,
            out_specs=pl.BlockSpec(memory_space=pltpu.VMEM),
            scratch_shapes=[
                pltpu.VMEM(stack, F32),
                pltpu.VMEM((2, chirp_len), BF16),
                pltpu.VMEM(stack, F32),
                pltpu.VMEM((rows,), jnp.int32),
                pltpu.VMEM((rows,), jnp.int32),
                pltpu.VMEM((taps, phases), F32),
                pltpu.VMEM((4, 2 * rows, 2 * rows), BF16),
                pltpu.VMEM((2, LANE, chirp_len + 2 * block), BF16),
                pltpu.VMEM((chirp_len + block, 2 * block), BF16),
                pltpu.VMEM((2 * rows, 3 * cells), BF16),
                pltpu.VMEM((rows, LANE), jnp.int32),
                pltpu.VMEM((taps, rows, LANE), F32),
                pltpu.VMEM((2 * rows, 2 * slots), BF16),
                pltpu.VMEM((2 * slots, 2 * rows), BF16),
                pltpu.VMEM(flat, BF16),
                pltpu.VMEM(tiles, BF16),
                pltpu.VMEM(tiles, BF16),
                pltpu.VMEM(flat, BF16),
                pltpu.VMEM((2 * rows, 3 * cells), F32),
                pltpu.VMEM(flat, BF16),
                pltpu.VMEM((PARTS, 2 * slots, part), BF16),
                pltpu.VMEM(flat, BF16),
                pltpu.VMEM((PARTS, 2 * slots, part), BF16),
                pltpu.VMEM((2 * rows, cells), BF16),
                pltpu.VMEM((2 * rows, cells), BF16),
                pltpu.VMEM(flat, BF16),
                pltpu.VMEM(tiles, BF16),
                pltpu.VMEM(tiles, BF16),
                pltpu.VMEM(flat, BF16),
                pltpu.SemaphoreType.DMA((7,)),
                pltpu.SemaphoreType.DMA((4 * PARTS,)),
                pltpu.SemaphoreType.DMA((4 * PARTS,)),
                pltpu.SemaphoreType.DMA((PASSED,)),
                pltpu.SemaphoreType.DMA((2, PARTS)),
                pltpu.SemaphoreType.DMA((2, PARTS)),
                pltpu.SemaphoreType.DMA((2, JOBS)),
                pltpu.SemaphoreType.DMA((2, JOBS)),
            ],
            compiler_params=pltpu.CompilerParams(
                collective_id=0, has_side_effects=True, vmem_limit_bytes=48 * 1024 * 1024
            ),
            cost_estimate=pl.CostEstimate(
                flops=1_600_000_000, bytes_accessed=2_000_000, transcendentals=0
            ),
        )(
            *(
                pltpu.with_memory_space_constraint(x, pltpu.HBM)
                for x in (
                    echo_field,
                    range_chirp,
                    azimuth_filter,
                    shifts,
                    tap_index,
                    taps_table.T,
                    trig,
                )
            )
        )

    placed = (P(None, "az", "rg"), P(), P(None, "az", "rg"), P("az"), P("az"), P())
    return jax.shard_map(
        local, mesh=mesh, in_specs=placed, out_specs=P(None, "az", "rg"), check_vma=False
    )
```

profile of v0, /device:TPU:1, one launch (start us, length us, event | category | flops | bytes accessed | tf_op | source)
XLA Modules:
  0.0 54.4 jit_solution(13844638319559459275)
XLA Ops:
  0.0 53.6 %shard_map.73 = f32[2,64,1024]{2,1,0:T(8,128)S(1)} custom-call(f32[2,64,1024]{2,1,0:T(8,128)} %echo_hbm.1, bf16[2,2048]{1,0:T(2,128)(2,1)} %chirp_hbm.1, f32[2,64,1024]{2,1,0:T(8,128)} %filt_hbm.1, s32[64]{0:T(128)} %shifts_hbm.1, s32[64]{0:T(128)} %tap_index_hbm.1, f32[8,16]{1,0:T(8,128)} %bitcast.1, bf16[32,4,128,128]{3,2,1,0:T(8,128)(2,1)} %constant.2.clone.trig_hbm), custom_call_target="tpu_custom_call" | custom-call | flops 1600000000 | bytes 2000000 | tf_op jit(solution)/shard_map/pallas_call | solution.py:587
  53.6 0.8 %copy.9 = f32[2,64,1024]{2,1,0:T(8,128)} copy(f32[2,64,1024]{2,1,0:T(8,128)S(1)} %shard_map.73) | data formatting | bytes 1048576
where the time goes:
time: 54.5 us; the launch traced here: 54.4 us
  Pallas kernels  53.6 us (98%)
  local copies, waits for them, and re-layouts  0.8 us (1%)
    pallas_call x1, Pallas kernels, local(): pl.pallas_call(functools.partial(kernel, n, ng, slots), out_shape=pltpu.V...  53.6 us

commit v1 on v0

--- a/solution.py
+++ b/solution.py
@@ -130,6 +130,7 @@
     band,
     weights,
     wide,
+    partial,
     shift_wide,
     coef_wide,
     spread,
@@ -158,7 +159,7 @@
     job_send,
     job_recv,
 ):
-    rows, cells = echo.shape[1], echo.shape[2]
+    rows, cells = filt.shape[1], filt.shape[2]
     chirp_len = chirp.shape[1]
     part = cells // PARTS
     lanes = part // LANE
@@ -173,13 +174,15 @@
         copy.start()
         return copy
 
-    echo_copy = fetch(echo_hbm, echo, 0)
+    echo_copies = [
+        fetch(echo_hbm.at[:, :, pl.ds(part * h, part)], echo.at[h], 6 + h) for h in range(PARTS)
+    ]
     chirp_copy = fetch(chirp_hbm, chirp, 1)
     shifts_copy = fetch(shifts_hbm, shifts, 2)
     index_copy = fetch(tap_index_hbm, tap_index, 3)
     table_copy = fetch(table_hbm, table, 4)
     trig_copy = fetch(trig_hbm.at[me], trig, 5)
-    filt_copy = fetch(filt_hbm, filt, 6)
+    filt_copy = fetch(filt_hbm, filt, 0)
 
     barrier = pltpu.get_barrier_semaphore()
 
@@ -192,15 +195,6 @@
     lax.fori_loop(1, n, greet, 0)
     for d in (1, 2, ng - 2, ng - 1):
         pl.semaphore_signal(barrier, inc=1, device_id=(me, lax.rem(g + d, ng)), device_id_type=MESH)
-
-    echo_copy.wait()
-    for s in range(groups):
-        at = slice(HALF * s, HALF * (s + 1))
-        wide[SUB * s : SUB * (s + 1), 0:cells] = jnp.concatenate(
-            [echo[0, at, :], echo[1, at, :]], axis=0
-        ).astype(BF16)
-
-    pl.semaphore_wait(barrier, n - 1 + 4)
 
     def halo_copy(src, dst, slot, d):
         return pltpu.make_async_remote_copy(
@@ -214,6 +208,11 @@
 
     odd = lax.rem(g, 2) == 1
 
+    even = lax.rem(g, 2) == 0
+
+    def later(h):
+        return h >= 2
+
     def sends_echo(d, h):
         far_enough = g >= d
         return far_enough & odd if d == 2 and h < PASSED else far_enough
@@ -238,9 +237,20 @@
             d,
         )
 
-    for d in (1, 2):
-        for h in range(PARTS):
-            pl.when(sends_echo(d, h))(echo_copy_of(d, h).start)
+    for h in range(PARTS):
+        echo_copies[h].wait()
+        for s in range(groups):
+            at = slice(HALF * s, HALF * (s + 1))
+            wide[SUB * s : SUB * (s + 1), part * h : part * (h + 1)] = jnp.concatenate(
+                [echo[h, 0, at, :], echo[h, 1, at, :]], axis=0
+            ).astype(BF16)
+        if h == 0:
+            pl.semaphore_wait(barrier, n - 1 + 4)
+        pl.when(sends_echo(1, h))(echo_copy_of(1, h).start)
+        if not later(h):
+            pl.when(sends_echo(2, h))(echo_copy_of(2, h).start)
+        else:
+            pl.when(sends_echo(2, h) & even)(echo_copy_of(2, h).start)
 
     chirp_copy.wait()
     span = chirp_len + 2 * block
@@ -311,14 +321,19 @@
     ny = n // nz
     my_y, my_z = lax.div(me, nz), lax.rem(me, nz)
     parity = lax.rem(me, 2)
-    spot = my_y * (nz // 2) + lax.div(my_z, 2)
 
     def away(i, count):
-        return count // 2 + (1 - 2 * lax.rem(i, 2)) * lax.div(i + 1, 2)
-
-    def tile(ref, p, at):
-        row = pl.multiple_of(SUB * lax.div(at, lanes), SUB)
-        col = pl.multiple_of(LANE * lax.rem(at, lanes), LANE)
+        return count // 2 + (1 - 2 * (i % 2)) * ((i + 1) // 2)
+
+    all_zs = [lax.rem(my_z + away(i, nz), nz) for i in range(nz)]
+
+    def place(y, z):
+        spot = lax.div(z, 2)
+        row = SUB * (nz // 2 // lanes) * y + SUB * lax.div(spot, lanes)
+        return pl.multiple_of(row, SUB), pl.multiple_of(LANE * lax.rem(spot, lanes), LANE)
+
+    def tile(ref, p):
+        row, col = place(my_y, my_z)
         return ref.at[p, pl.ds(row, SUB), pl.ds(col, LANE)]
 
     def other(p):
@@ -327,46 +342,62 @@
     def scatter(src, dst, phase, p):
         job = p // JOBS
 
-        def start(k, carry):
-            y = lax.rem(my_y + away(lax.rem(k, ny), ny), ny)
-            z = lax.rem(my_z + 2 * away(lax.div(k, ny), nz // 2) + other(p), nz)
+        def send(y, z):
+            row, col = place(y, z)
             pltpu.make_async_remote_copy(
-                src_ref=tile(src, p, y * (nz // 2) + lax.div(z, 2)),
+                src_ref=src.at[p, pl.ds(row, SUB), pl.ds(col, LANE)],
                 dst_ref=dst.at[job, me],
                 send_sem=part_send.at[phase, p],
                 recv_sem=job_recv.at[phase, job],
                 device_id=(y * nz + z, g),
                 device_id_type=MESH,
             ).start()
+
+        zs = [lax.rem(my_z + 2 * away(i, nz // 2) + other(p), nz) for i in range(nz // 2)]
+
+        def start(k, carry):
+            y = lax.rem(my_y + away(k, ny), ny)
+            for z in zs:
+                send(y, z)
             return carry
 
-        lax.fori_loop(0, n // 2 - 1 + other(p), start, 0)
+        lax.fori_loop(0, ny - 1, start, 0)
+        for z in zs[:-1]:
+            send(my_y, z)
+        pl.when(other(p) == 1)(lambda: send(my_y, zs[-1]))
 
         @pl.when(other(p) == 0)
         def _():
             pltpu.make_async_copy(
-                tile(src, p, spot), dst.at[job, me], job_recv.at[phase, job]
+                tile(src, p), dst.at[job, me], job_recv.at[phase, job]
             ).start()
 
     def gather(src, dst, phase, job):
         p = 2 * job + parity
 
-        def start(k, carry):
-            y = lax.rem(my_y + away(lax.rem(k, ny), ny), ny)
-            z = lax.rem(my_z + away(lax.div(k, ny), nz), nz)
+        target = tile(dst, p)
+
+        def send(y, z):
             q = y * nz + z
             pltpu.make_async_remote_copy(
                 src_ref=src.at[job, q],
-                dst_ref=tile(dst, p, spot),
+                dst_ref=target,
                 send_sem=job_send.at[phase, job],
                 recv_sem=part_recv.at[phase, p],
                 device_id=(q, g),
                 device_id_type=MESH,
             ).start()
+
+        def start(k, carry):
+            y = lax.rem(my_y + away(k, ny), ny)
+            for z in all_zs:
+                send(y, z)
             return carry
 
-        lax.fori_loop(0, n - 1, start, 0)
-        pltpu.make_async_copy(src.at[job, me], tile(dst, p, spot), part_recv.at[phase, p]).start()
+        lax.fori_loop(0, ny - 1, start, 0)
+        for z in all_zs[:-1]:
+            send(my_y, z)
+        pltpu.make_async_copy(src.at[job, me], target, part_recv.at[phase, p]).start()
 
     def scattered(dst, phase, job):
         pltpu.make_async_copy(dst.at[job], dst.at[job], job_recv.at[phase, job]).wait()
@@ -382,9 +413,19 @@
         for p, (re, im) in enumerate(fft(xs)):
             dst[h, p] = encode(jnp.concatenate([re, im], axis=0) * (1.0 / math.sqrt(n)))
 
+    def compress_near(h):
+        reach = 2 * cells - part * h
+        partial[h] = jnp.dot(
+            wide[:, part * h : 2 * cells], weights[:reach, :], preferred_element_type=F32
+        )
+
     def compress(h):
-        left = wide[:, part * h : part * h + chirp_len + block]
-        product = jnp.dot(left, weights[...], preferred_element_type=F32)
+        reach = 2 * cells - part * h
+        product = partial[h] + jnp.dot(
+            wide[:, 2 * cells : part * h + chirp_len + block],
+            weights[reach:, :],
+            preferred_element_type=F32,
+        )
         piece = product.reshape(groups, 2, HALF, 2 * block)
         real = piece[:, 0, :, :block] - piece[:, 1, :, block:]
         imag = piece[:, 0, :, block:] + piece[:, 1, :, :block]
@@ -402,7 +443,12 @@
         echo_arrived(1, h)
         if h < PASSED:
             pl.when(passes_on)(pass_on(h).start)
+        if h == 0:
+            for i in range(PARTS):
+                if later(i):
+                    pl.when(sends_echo(2, i) & odd)(echo_copy_of(2, i).start)
     for h in range(PARTS):
+        compress_near(h)
         echo_arrived(2, h)
         compress(h)
         scatter(send_1, recv_1, 0, h)
@@ -529,14 +575,14 @@
     for h in range(PARTS):
         spec_arrived(1, h)
     filt_copy.wait()
-    for half in range(2):
-        for h in range(PARTS // 2 * half, PARTS // 2 * (half + 1)):
+    for h in range(PARTS):
+        if h % 2 == 0:
             spec_arrived(2, h)
-        migrate(half)
-        for h in range(PARTS // 2 * half, PARTS // 2 * (half + 1)):
-            col = slice(part * h, part * (h + 1))
-            send_3[h] = encode(times(2, high[:, col], low[:, col]))
-            scatter(send_3, recv_3, 1, h)
+            spec_arrived(2, h + 1)
+            migrate(h // 2)
+        col = slice(part * h, part * (h + 1))
+        send_3[h] = encode(times(2, high[:, col], low[:, col]))
+        scatter(send_3, recv_3, 1, h)
 
     for job in range(JOBS):
         scattered(recv_3, 1, job)
@@ -590,7 +636,7 @@
             in_specs=[hbm] * 7,
             out_specs=pl.BlockSpec(memory_space=pltpu.VMEM),
             scratch_shapes=[
-                pltpu.VMEM(stack, F32),
+                pltpu.VMEM((PARTS, 2, rows, part), F32),
                 pltpu.VMEM((2, chirp_len), BF16),
                 pltpu.VMEM(stack, F32),
                 pltpu.VMEM((rows,), jnp.int32),
@@ -600,6 +646,7 @@
                 pltpu.VMEM((2, LANE, chirp_len + 2 * block), BF16),
                 pltpu.VMEM((chirp_len + block, 2 * block), BF16),
                 pltpu.VMEM((2 * rows, 3 * cells), BF16),
+                pltpu.VMEM((PARTS, 2 * rows, 2 * block), F32),
                 pltpu.VMEM((rows, LANE), jnp.int32),
                 pltpu.VMEM((taps, rows, LANE), F32),
                 pltpu.VMEM((2 * rows, 2 * slots), BF16),
@@ -619,7 +666,7 @@
                 pltpu.VMEM(tiles, BF16),
                 pltpu.VMEM(tiles, BF16),
                 pltpu.VMEM(flat, BF16),
-                pltpu.SemaphoreType.DMA((7,)),
+                pltpu.SemaphoreType.DMA((6 + PARTS,)),
                 pltpu.SemaphoreType.DMA((4 * PARTS,)),
                 pltpu.SemaphoreType.DMA((4 * PARTS,)),
                 pltpu.SemaphoreType.DMA((PASSED,)),

time: 54.5 us -> 53.5 us (0.982)
  Pallas kernels: 53.6 us -> 52.2 us
    pallas_call x1, Pallas kernels: 53.6 us -> 52.2 us  [local(): pl.pallas_call(functools.partial(kernel, n, ng, slots), out_shape=pltpu.V...]
where the time goes in v1:
time: 53.5 us; the launch traced here: 53 us
  Pallas kernels  52.2 us (98%)
  local copies, waits for them, and re-layouts  0.8 us (1%)
    pallas_call x1, Pallas kernels, local(): pl.pallas_call(functools.partial(kernel, n, ng, slots), out_shape=pltpu.V...  52.2 us

profile of v1, /device:TPU:1, one launch (start us, length us, event | category | flops | bytes accessed | tf_op | source)
XLA Modules:
  0.0 53.0 jit_solution(2210757647987146964)
XLA Ops:
  0.0 52.2 %shard_map.73 = f32[2,64,1024]{2,1,0:T(8,128)S(1)} custom-call(f32[2,64,1024]{2,1,0:T(8,128)} %echo_hbm.1, bf16[2,2048]{1,0:T(2,128)(2,1)} %chirp_hbm.1, f32[2,64,1024]{2,1,0:T(8,128)} %filt_hbm.1, s32[64]{0:T(128)} %shifts_hbm.1, s32[64]{0:T(128)} %tap_index_hbm.1, f32[8,16]{1,0:T(8,128)} %bitcast.1, bf16[32,4,128,128]{3,2,1,0:T(8,128)(2,1)} %constant.2.clone.trig_hbm), custom_call_target="tpu_custom_call" | custom-call | flops 1600000000 | bytes 2000000 | tf_op jit(solution)/shard_map/pallas_call | solution.py:633
  52.3 0.8 %copy.9 = f32[2,64,1024]{2,1,0:T(8,128)} copy(f32[2,64,1024]{2,1,0:T(8,128)S(1)} %shard_map.73) | data formatting | bytes 1048576

commit v2 on v1

--- a/solution.py
+++ b/solution.py
@@ -158,6 +158,8 @@
     part_recv,
     job_send,
     job_recv,
+    round_1,
+    round_2,
 ):
     rows, cells = filt.shape[1], filt.shape[2]
     chirp_len = chirp.shape[1]
@@ -177,24 +179,32 @@
     echo_copies = [
         fetch(echo_hbm.at[:, :, pl.ds(part * h, part)], echo.at[h], 6 + h) for h in range(PARTS)
     ]
+
+    ny = n // nz
+    my_y, my_z = lax.div(me, nz), lax.rem(me, nz)
+    def away(i, count):
+        return count // 2 + (1 - 2 * (i % 2)) * ((i + 1) // 2)
+
+    all_zs = [lax.rem(my_z + away(i, nz), nz) for i in range(nz)]
+    barrier = pltpu.get_barrier_semaphore()
+
+    near = [(lax.rem(my_y + d, ny), my_z) for d in range(1, ny)]
+    near = near + [(my_y, lax.rem(my_z + d, nz)) for d in (1, 2, nz - 2, nz - 1)]
+
+    def tell(semaphore):
+        for y, z in near:
+            pl.semaphore_signal(semaphore, inc=1, device_id=(y * nz + z, g), device_id_type=MESH)
+
+    for d in (1, 2, ng - 2, ng - 1):
+        pl.semaphore_signal(barrier, inc=1, device_id=(me, lax.rem(g + d, ng)), device_id_type=MESH)
+    tell(barrier)
+
     chirp_copy = fetch(chirp_hbm, chirp, 1)
     shifts_copy = fetch(shifts_hbm, shifts, 2)
     index_copy = fetch(tap_index_hbm, tap_index, 3)
     table_copy = fetch(table_hbm, table, 4)
     trig_copy = fetch(trig_hbm.at[me], trig, 5)
     filt_copy = fetch(filt_hbm, filt, 0)
-
-    barrier = pltpu.get_barrier_semaphore()
-
-    def greet(k, carry):
-        pl.semaphore_signal(
-            barrier, inc=1, device_id=(lax.rem(me + k, n), g), device_id_type=MESH
-        )
-        return carry
-
-    lax.fori_loop(1, n, greet, 0)
-    for d in (1, 2, ng - 2, ng - 1):
-        pl.semaphore_signal(barrier, inc=1, device_id=(me, lax.rem(g + d, ng)), device_id_type=MESH)
 
     def halo_copy(src, dst, slot, d):
         return pltpu.make_async_remote_copy(
@@ -245,7 +255,8 @@
                 [echo[h, 0, at, :], echo[h, 1, at, :]], axis=0
             ).astype(BF16)
         if h == 0:
-            pl.semaphore_wait(barrier, n - 1 + 4)
+            pl.semaphore_wait(barrier, 4 + len(near))
+            tell(round_1)
         pl.when(sends_echo(1, h))(echo_copy_of(1, h).start)
         if not later(h):
             pl.when(sends_echo(2, h))(echo_copy_of(2, h).start)
@@ -273,6 +284,9 @@
                 c, :, start : start + block
             ]
 
+    pl.semaphore_wait(round_1, len(near))
+    tell(round_2)
+
     shifts_copy.wait()
     index_copy.wait()
     table_copy.wait()
@@ -318,14 +332,7 @@
     spread[...] = matches.astype(BF16)
     gathering[...] = matches.T.astype(BF16)
 
-    ny = n // nz
-    my_y, my_z = lax.div(me, nz), lax.rem(me, nz)
     parity = lax.rem(me, 2)
-
-    def away(i, count):
-        return count // 2 + (1 - 2 * (i % 2)) * ((i + 1) // 2)
-
-    all_zs = [lax.rem(my_z + away(i, nz), nz) for i in range(nz)]
 
     def place(y, z):
         spot = lax.div(z, 2)
@@ -447,6 +454,7 @@
             for i in range(PARTS):
                 if later(i):
                     pl.when(sends_echo(2, i) & odd)(echo_copy_of(2, i).start)
+    pl.semaphore_wait(round_2, len(near))
     for h in range(PARTS):
         compress_near(h)
         echo_arrived(2, h)
@@ -674,6 +682,8 @@
                 pltpu.SemaphoreType.DMA((2, PARTS)),
                 pltpu.SemaphoreType.DMA((2, JOBS)),
                 pltpu.SemaphoreType.DMA((2, JOBS)),
+                pltpu.SemaphoreType.REGULAR,
+                pltpu.SemaphoreType.REGULAR,
             ],
             compiler_params=pltpu.CompilerParams(
                 collective_id=0, has_side_effects=True, vmem_limit_bytes=48 * 1024 * 1024

time: 53.5 us -> 51.3 us (0.959)
  Pallas kernels: 52.2 us -> 50.4 us
    pallas_call x1, Pallas kernels: 52.2 us -> 50.4 us  [local(): pl.pallas_call(functools.partial(kernel, n, ng, slots), out_shape=pltpu.V...]
where the time goes in v2:
time: 51.3 us; the launch traced here: 51.2 us
  Pallas kernels  50.4 us (98%)
  local copies, waits for them, and re-layouts  0.8 us (2%)
    pallas_call x1, Pallas kernels, local(): pl.pallas_call(functools.partial(kernel, n, ng, slots), out_shape=pltpu.V...  50.4 us

profile of v2, /device:TPU:1, one launch (start us, length us, event | category | flops | bytes accessed | tf_op | source)
XLA Modules:
  0.0 51.2 jit_solution(4585502293869474313)
XLA Ops:
  0.0 50.4 %shard_map.73 = f32[2,64,1024]{2,1,0:T(8,128)S(1)} custom-call(f32[2,64,1024]{2,1,0:T(8,128)} %echo_hbm.1, bf16[2,2048]{1,0:T(2,128)(2,1)} %chirp_hbm.1, f32[2,64,1024]{2,1,0:T(8,128)} %filt_hbm.1, s32[64]{0:T(128)} %shifts_hbm.1, s32[64]{0:T(128)} %tap_index_hbm.1, f32[8,16]{1,0:T(8,128)} %bitcast.1, bf16[32,4,128,128]{3,2,1,0:T(8,128)(2,1)} %constant.2.clone.trig_hbm), custom_call_target="tpu_custom_call" | custom-call | flops 1600000000 | bytes 2000000 | tf_op jit(solution)/shard_map/pallas_call | solution.py:641
  50.4 0.8 %copy.9 = f32[2,64,1024]{2,1,0:T(8,128)} copy(f32[2,64,1024]{2,1,0:T(8,128)S(1)} %shard_map.73) | data formatting | bytes 1048576

commit v3 on v2

--- a/solution.py
+++ b/solution.py
@@ -176,10 +176,6 @@
         copy.start()
         return copy
 
-    echo_copies = [
-        fetch(echo_hbm.at[:, :, pl.ds(part * h, part)], echo.at[h], 6 + h) for h in range(PARTS)
-    ]
-
     ny = n // nz
     my_y, my_z = lax.div(me, nz), lax.rem(me, nz)
     def away(i, count):
@@ -188,16 +184,21 @@
     all_zs = [lax.rem(my_z + away(i, nz), nz) for i in range(nz)]
     barrier = pltpu.get_barrier_semaphore()
 
-    near = [(lax.rem(my_y + d, ny), my_z) for d in range(1, ny)]
-    near = near + [(my_y, lax.rem(my_z + d, nz)) for d in (1, 2, nz - 2, nz - 1)]
+    near = [(lax.rem(my_y + d, ny), my_z) for d in (2, 1, ny - 1)]
+    near = [(my_y, lax.rem(my_z + d, nz)) for d in (2, nz - 2)] + near
+    near = near + [(my_y, lax.rem(my_z + d, nz)) for d in (1, nz - 1)]
 
     def tell(semaphore):
         for y, z in near:
             pl.semaphore_signal(semaphore, inc=1, device_id=(y * nz + z, g), device_id_type=MESH)
 
+    tell(barrier)
     for d in (1, 2, ng - 2, ng - 1):
         pl.semaphore_signal(barrier, inc=1, device_id=(me, lax.rem(g + d, ng)), device_id_type=MESH)
-    tell(barrier)
+
+    echo_copies = [
+        fetch(echo_hbm.at[:, :, pl.ds(part * h, part)], echo.at[h], 6 + h) for h in range(PARTS)
+    ]
 
     chirp_copy = fetch(chirp_hbm, chirp, 1)
     shifts_copy = fetch(shifts_hbm, shifts, 2)
@@ -221,7 +222,7 @@
     even = lax.rem(g, 2) == 0
 
     def later(h):
-        return h >= 2
+        return h >= 1
 
     def sends_echo(d, h):
         far_enough = g >= d

time: 51.3 us -> 50.9 us (level)
  no operation moved by 1% of the time
where the time goes in v3:
time: 50.9 us; the launch traced here: 50.8 us
  Pallas kernels  50 us (98%)
  local copies, waits for them, and re-layouts  0.8 us (2%)
    pallas_call x1, Pallas kernels, local(): pl.pallas_call(functools.partial(kernel, n, ng, slots), out_shape=pltpu.V...  50 us

profile of v3, /device:TPU:1, one launch (start us, length us, event | category | flops | bytes accessed | tf_op | source)
XLA Modules:
  0.0 50.8 jit_solution(896820788148116735)
XLA Ops:
  0.0 50.0 %shard_map.73 = f32[2,64,1024]{2,1,0:T(8,128)S(1)} custom-call(f32[2,64,1024]{2,1,0:T(8,128)} %echo_hbm.1, bf16[2,2048]{1,0:T(2,128)(2,1)} %chirp_hbm.1, f32[2,64,1024]{2,1,0:T(8,128)} %filt_hbm.1, s32[64]{0:T(128)} %shifts_hbm.1, s32[64]{0:T(128)} %tap_index_hbm.1, f32[8,16]{1,0:T(8,128)} %bitcast.1, bf16[32,4,128,128]{3,2,1,0:T(8,128)(2,1)} %constant.2.clone.trig_hbm), custom_call_target="tpu_custom_call" | custom-call | flops 1600000000 | bytes 2000000 | tf_op jit(solution)/shard_map/pallas_call | solution.py:642
  50.0 0.8 %copy.9 = f32[2,64,1024]{2,1,0:T(8,128)} copy(f32[2,64,1024]{2,1,0:T(8,128)S(1)} %shard_map.73) | data formatting | bytes 1048576

commit v4 on v3

--- a/solution.py
+++ b/solution.py
@@ -257,12 +257,13 @@
             ).astype(BF16)
         if h == 0:
             pl.semaphore_wait(barrier, 4 + len(near))
-            tell(round_1)
         pl.when(sends_echo(1, h))(echo_copy_of(1, h).start)
         if not later(h):
             pl.when(sends_echo(2, h))(echo_copy_of(2, h).start)
         else:
             pl.when(sends_echo(2, h) & even)(echo_copy_of(2, h).start)
+        if h == 1:
+            tell(round_1)
 
     chirp_copy.wait()
     span = chirp_len + 2 * block

time: 50.9 us -> 51.1 us (level)
  no operation moved by 1% of the time
where the time goes in v4:
time: 51.1 us
  Pallas kernels  50.2 us (98%)
  local copies, waits for them, and re-layouts  0.8 us (2%)
    pallas_call x1, Pallas kernels, local(): pl.pallas_call(functools.partial(kernel, n, ng, slots), out_shape=pltpu.V...  50.2 us

profile of v4, /device:TPU:1, one launch (start us, length us, event | category | flops | bytes accessed | tf_op | source)
XLA Modules:
  0.0 51.1 jit_solution(11476979240153711167)
XLA Ops:
  0.0 50.2 %shard_map.73 = f32[2,64,1024]{2,1,0:T(8,128)S(1)} custom-call(f32[2,64,1024]{2,1,0:T(8,128)} %echo_hbm.1, bf16[2,2048]{1,0:T(2,128)(2,1)} %chirp_hbm.1, f32[2,64,1024]{2,1,0:T(8,128)} %filt_hbm.1, s32[64]{0:T(128)} %shifts_hbm.1, s32[64]{0:T(128)} %tap_index_hbm.1, f32[8,16]{1,0:T(8,128)} %bitcast.1, bf16[32,4,128,128]{3,2,1,0:T(8,128)(2,1)} %constant.2.clone.trig_hbm), custom_call_target="tpu_custom_call" | custom-call | flops 1600000000 | bytes 2000000 | tf_op jit(solution)/shard_map/pallas_call | solution.py:643
  50.3 0.8 %copy.9 = f32[2,64,1024]{2,1,0:T(8,128)} copy(f32[2,64,1024]{2,1,0:T(8,128)S(1)} %shard_map.73) | data formatting | bytes 1048576
